TPU v7x, 128 devices: a whole 4x4x4 slice. The times are simulated.
128 devices in a mesh: pa: 32 (over x, z, core), mu: 4 (over y).
Axes of the slice: x: 4, y: 4, z: 4, core: 2. Of those that a mesh axis runs over, the one named last changes fastest.
Arguments:
- tensor: bfloat16 [1536, 512, 512], P('pa'), may hold values from -6 to 6
- block_mask: int32 [24, 8, 8], replicated, may hold values from 0 to 1, as said below
- group_of_block: int32 [8], replicated, may hold values from 0 to 3, never falling along the last dimension, each value on 1 to 3 neighbouring positions
- green_occ: bfloat16 [512, 512], replicated, may hold values from -0.25 to 0.25
- green_virt: bfloat16 [512, 512], replicated, may hold values from -0.25 to 0.25
Outputs:
- chi: float32 [1536, 1536], P('pa', 'mu')
Inputs may be any that keep to these rules, and one draw needn't show every extreme that they name: `block_mask`: entries are 0 or 1; the share of ones differs from one RI block to another. `group_of_block`: group numbers never fall along the AO blocks; each group holds 1 to 3 blocks.
All inputs are finite; a program needn't handle non-finite values.
Results may differ from a plain program's by a relative error of at most 0.004.
Values may be sent and summed in bfloat16 or wider, within the bound.
A program may use at most 192 MiB of HBM per device.

v0:
```python
import jax
import jax.numpy as jnp
from jax import lax
from jax.sharding import PartitionSpec as P

BS = 64
GROUP_REACH = 1


def shards(tensor, block_mask, group_of_block, green_occ, green_virt):
    p_rows = tensor.shape[0]
    nao = tensor.shape[2]
    nab = nao // BS
    n_mu = lax.axis_size("mu")
    lam = nao // n_mu
    row_index = lax.axis_index("pa")
    col_index = lax.axis_index("mu")
    nblocks = block_mask.shape[0]
    global_rows = row_index * p_rows + jnp.arange(p_rows, dtype=jnp.int32)
    onehot = ((global_rows // BS)[:, None] == jnp.arange(nblocks, dtype=jnp.int32)[None, :]).astype(
        jnp.float32
    )
    mask_rows = jnp.dot(onehot, block_mask.reshape(nblocks, nab * nab).astype(jnp.float32)).reshape(
        p_rows, nab, nab
    )
    expanded = jnp.repeat(mask_rows, BS, axis=2).astype(jnp.bfloat16)
    masked = (tensor.reshape(p_rows, nab, BS, nao) * expanded[:, :, None, :]).reshape(
        p_rows, nao, nao
    )
    groups = jnp.repeat(group_of_block, BS)
    keep = (jnp.abs(groups[:, None] - groups[None, :]) <= GROUP_REACH).astype(jnp.bfloat16)
    occ = green_occ * keep
    virt = green_virt * keep
    occ_cols = lax.dynamic_slice_in_dim(occ, col_index * lam, lam, 1)
    own_rows = lax.dynamic_slice_in_dim(masked, col_index * lam, lam, 1).reshape(p_rows, lam * nao)
    half = jnp.einsum("ml,pmn->pln", occ_cols, masked, preferred_element_type=jnp.float32)
    half = half.astype(jnp.bfloat16)
    product = jnp.einsum("pln,ns->pls", half, virt, preferred_element_type=jnp.float32).astype(
        jnp.bfloat16
    )
    product = product.reshape(p_rows, lam * nao)
    product_full, tensor_full = (
        lax.all_to_all(product, "pa", split_axis=1, concat_axis=0, tiled=True),
        lax.all_to_all(own_rows, "pa", split_axis=1, concat_axis=0, tiled=True),
    )
    scale = 1.0 / nao
    term = (
        lax.dot_general(
            product_full, tensor_full, (((1,), (1,)), ((), ())), preferred_element_type=jnp.float32
        )
        * scale
    )
    row_part = lax.psum_scatter(term, "pa", scatter_dimension=0, tiled=True)
    tile = lax.psum_scatter(row_part, "mu", scatter_dimension=1, tiled=True)
    return tile


def solution(mesh):
    placed = (P("pa", None, None), P(), P(), P(), P())
    return jax.shard_map(
        shards, mesh=mesh, in_specs=placed, out_specs=P("pa", "mu"), check_vma=False
    )
```

profile of v0, /device:TPU:0, one launch (start us, length us, event | category | flops | bytes accessed | tf_op | source)
XLA Modules:
  0.0 380.2 jit_solution(12028284092424519537)
XLA Ops:
  6.5 0.7 broadcast_in_dim.10
  7.3 0.1 sub.22
  7.3 0.9 convolution_convert_fusion
  8.2 0.1 copy.14
  8.4 0.3 abs_compare_fusion
  8.7 0.5 broadcast_in_dim.4
  9.2 0.5 convert_element_type.31
  9.6 0.0 copy-start
  9.7 20.6 %bitcast_multiply_fusion = bf16[48,512,512]{2,1,0:T(8,128)(2,1)} fusion(bf16[48,512,512]{2,1,0:T(8,128)(2,1)} %param.5, bf16[48,8,512]{2,1,0:T(8,128)(2,1)S(1)} %convert_element_type.31), kind=kLoop, calls=%fused_computation | loop fusion | flops 12582912 | bytes 50724864 | tf_op jit(solution)/shard_map/mul | solution.py:27
  30.2 0.0 copy-done
  30.2 19.4 %fusion.5 = bf16[48,128,512]{2,1,0:T(8,128)(2,1)} fusion(bf16[48,512,512]{2,1,0:T(8,128)(2,1)} %bitcast_multiply_fusion, pred[512,512]{1,0:T(32,128)(4,1)S(1)} %abs_compare_fusion, bf16[512,512]{1,0:T(8,128)(2,1)S(1)} %copy-done, s32[]{:T(128)S(6)} %select_n.14, bf16[512,512]{1,0:T(8,128)(2,1)} %param.8), kind=kOutput, calls=%fused_computation.6 | convolution fusion | flops 6449070080 | bytes 32440324 | tf_op jit(solution)/shard_map/pln,ns->pls/dot_general | solution.py:38
  49.6 10.7 %all_to_all.28 = bf16[48,32,2048]{2,1,0:T(8,128)(2,1)} reshape(bf16[48,128,512]{2,1,0:T(8,128)(2,1)} %fusion.5) | data formatting | bytes 12582912 | tf_op jit(solution)/shard_map/all_to_all | solution.py:43
  60.3 8.9 %copy.17 = bf16[48,32,2048]{2,0,1:T(8,128)(2,1)} copy(bf16[48,32,2048]{2,1,0:T(8,128)(2,1)} %all_to_all.28) | data formatting | bytes 12582912 | tf_op jit(solution)/shard_map/all_to_all | solution.py:43
  69.3 8.4 %all-to-all-start = ((bf16[48,32,2048]{2,0,1:T(8,128)(2,1)}), bf16[48,32,2048]{2,0,1:T(8,128)(2,1)}, u32[]{:S(2)}, u32[]{:S(2)}) async-start(bf16[48,32,2048]{2,0,1:T(8,128)(2,1)} %copy.17), calls=%async_computation | async-start | bytes 12582912 | tf_op jit(solution)/shard_map/all_to_all | solution.py:43
  77.6 0.0 reduce-scatter.3.cloned.1.call-start
  77.7 6.1 %constant_dynamic-slice_fusion = bf16[48,128,512]{2,1,0:T(8,128)(2,1)} fusion(bf16[48,512,512]{2,1,0:T(8,128)(2,1)} %bitcast_multiply_fusion, s32[]{:T(128)S(6)} %select_n.14), kind=kLoop, calls=%fused_computation.25 | loop fusion | bytes 12582916 | tf_op jit(solution)/shard_map/dynamic_slice | solution.py:35
  83.8 10.7 %all_to_all.32 = bf16[48,32,2048]{2,1,0:T(8,128)(2,1)} reshape(bf16[48,128,512]{2,1,0:T(8,128)(2,1)} %constant_dynamic-slice_fusion) | data formatting | bytes 12582912 | tf_op jit(solution)/shard_map/all_to_all | solution.py:44
  94.5 8.9 %copy.18 = bf16[48,32,2048]{2,0,1:T(8,128)(2,1)} copy(bf16[48,32,2048]{2,1,0:T(8,128)(2,1)} %all_to_all.32) | data formatting | bytes 12582912 | tf_op jit(solution)/shard_map/all_to_all | solution.py:44
  103.4 54.1 %all-to-all-done = bf16[48,32,2048]{2,0,1:T(8,128)(2,1)} async-done(((bf16[48,32,2048]{2,0,1:T(8,128)(2,1)}), bf16[48,32,2048]{2,0,1:T(8,128)(2,1)}, u32[]{:S(2)}, u32[]{:S(2)}) %all-to-all-start) | async-done | bytes 6291488 | tf_op jit(solution)/shard_map/all_to_all | solution.py:43
  157.5 85.6 %all_to_all.38 = bf16[48,32,2048]{2,0,1:T(8,128)(2,1)S(1)} all-to-all(bf16[48,32,2048]{2,0,1:T(8,128)(2,1)} %copy.18), channel_id=1, replica_groups=mesh['pa'=32,'mu'=4] {'pa'}, dimensions={1} | all-to-all | bytes 12582912 | tf_op jit(solution)/shard_map/all_to_all | solution.py:44
  243.1 13.7 %convolution_multiply_fusion = f32[1536,1536]{1,0:T(8,128)} fusion(bf16[1536,2048]{1,0:T(8,128)(2,1)} %bitcast.9, bf16[1536,2048]{1,0:T(8,128)(2,1)S(1)} %bitcast.35), kind=kOutput, calls=%fused_computation.1 | convolution fusion | flops 9666035712 | bytes 22020096 | tf_op jit(solution)/shard_map/dot_general | solution.py:48
  256.8 0.0 reduce-scatter.3.cloned.1.call-update
  256.8 0.0 reduce-scatter.5.cloned.1.call-start
  256.9 93.9 %reduce-scatter.3.cloned.1.call-done = f32[48,1536]{1,0:T(8,128)} async-done(((f32[1536,1536]{1,0:T(8,128)}), f32[48,1536]{1,0:T(8,128)}) %reduce-scatter.3.cloned.1.call-update) | async-done | bytes 294928 | tf_op jit(solution)/shard_map/reduce_scatter | solution.py:53
  350.8 0.0 reduce-scatter.5.cloned.1.call-update
  350.8 22.5 %reduce-scatter.5.cloned.1.call-done = f32[48,384]{1,0:T(8,128)} async-done(((f32[48,1536]{1,0:T(8,128)}), f32[48,384]{1,0:T(8,128)}) %reduce-scatter.5.cloned.1.call-update) | async-done | bytes 73744 | tf_op jit(solution)/shard_map/reduce_scatter | solution.py:54
  (1 shorter events, 0.0 us)
Async XLA Ops:
  9.6 20.6 %copy-start = (bf16[512,512]{1,0:T(8,128)(2,1)S(1)}, bf16[512,512]{1,0:T(8,128)(2,1)}, u32[]{:S(2)}) copy-start(bf16[512,512]{1,0:T(8,128)(2,1)} %param.9) | copy-start | bytes 1572868
  69.3 88.2 %all-to-all-start = ((bf16[48,32,2048]{2,0,1:T(8,128)(2,1)}), bf16[48,32,2048]{2,0,1:T(8,128)(2,1)}, u32[]{:S(2)}, u32[]{:S(2)}) async-start(bf16[48,32,2048]{2,0,1:T(8,128)(2,1)} %copy.17), calls=%async_computation | async-start | bytes 12582912 | tf_op jit(solution)/shard_map/all_to_all | solution.py:43
  77.6 273.2 %reduce-scatter.3.cloned.1.call-start = ((), (), s32[]{:S(2)}) async-start(), calls=%async_computation.4 | async-start | bytes 9732096 | tf_op jit(solution)/shard_map/reduce_scatter | solution.py:53
  256.8 116.5 %reduce-scatter.5.cloned.1.call-start = ((), (), s32[]{:S(2)}) async-start(), calls=%async_computation.5 | async-start | bytes 368640 | tf_op jit(solution)/shard_map/reduce_scatter | solution.py:54
Sparse Core Ops, SparseCore 0:
  256.9 93.8 reduce-scatter.2
  353.3 19.9 reduce-scatter.4
where the time goes:
time: 381 us; the launch traced here: 380 us
  waiting for transfers between devices  171 us (45%)
  blocking collectives  85.6 us (22%)
  local copies, waits for them, and re-layouts  47.2 us (12%)
  matrix products  34 us (9%)
  other arithmetic  20.9 us (5%)
  between operations  13.5 us (4%)
  starting transfers between devices  8.45 us (2%)
    reduce_scatter x1, waiting for transfers between devices, shards(): row_part = lax.psum_scatter(term, 'pa', scatter_dimension=0, tiled=True)  93.9 us
    all_to_all x1, blocking collectives, shards(): lax.all_to_all(own_rows, 'pa', split_axis=1, concat_axis=0, tiled=True)  85.6 us
    all_to_all x1, waiting for transfers between devices, shards(): lax.all_to_all(product, 'pa', split_axis=1, concat_axis=0, tiled=True)  54.1 us
    reduce_scatter x1, waiting for transfers between devices, shards(): tile = lax.psum_scatter(row_part, 'mu', scatter_dimension=1, tiled=True)  22.5 us
    mul x1, other arithmetic, shards(): tensor.reshape(p_rows, nab, BS, nao) * expanded[:, :, None, :]  20.6 us
    all_to_all x2, local copies, waits for them, and re-layouts, shards(): lax.all_to_all(product, 'pa', split_axis=1, concat_axis=0, tiled=True)  19.7 us
    all_to_all x2, local copies, waits for them, and re-layouts, shards(): lax.all_to_all(own_rows, 'pa', split_axis=1, concat_axis=0, tiled=True)  19.6 us
    dot_general x1, matrix products, shards(): jnp.einsum('pln,ns->pls', half, virt, preferred_element_type=jnp.float32)  19.4 us
  transfers between devices with their start and end apart: 3, of which 3 were waited for; matrix products, arithmetic and copies ran while one was open for 4% of the time, Pallas kernels for 0%

commit v1 on v0

v1 whole, which is shorter than its diff:
```python
import jax
import jax.numpy as jnp
from jax import lax
from jax.experimental import pallas as pl
from jax.experimental.pallas import tpu as pltpu
from jax.sharding import PartitionSpec as P

MESH = pl.DeviceIdType.MESH
F32, BF16 = jnp.float32, jnp.bfloat16

BS = 64
GROUP_REACH = 1
NX = NZ = NY = 4
CHIPS = NX * NZ
ROWS = 48
NP = 1536
NAO = 512
LB = 16
SB = 128
KC = LB * SB
XW = 3
XR = ROWS // XW
YW = 6
YR = ROWS // YW
WR = CHIPS * YR
QC = NP // NY
NEAR = [(1, 0), (0, 1), (-1, 0), (0, -1), (1, 1), (-1, -1), (1, -1), (-1, 1), (2, 0), (0, 2), (2, 1), (1, 2), (2, -1), (-1, 2), (2, 2)]
DY = (2, 1, 3)


def block_of(shape, dim, first=0):
    return lax.broadcasted_iota(jnp.int32, shape, dim) // BS + first


def kernel(
    tensor, mask, group, occ, virt, out,
    xr, xl, tb, me, occ_t, vm, mv, perm, half, ys, yr, yl, cb, sb, yrs, zr,
    x_send, x_recv, l_send, l_recv, t_sem, y_send, y_recv, c_send, c_recv, z_send, z_recv,
):
    pa, mu = lax.axis_index("pa"), lax.axis_index("mu")
    x, z, core = pa // (2 * NZ), lax.rem(pa // 2, NZ), lax.rem(pa, 2)
    chip = x * NZ + z

    def moved(dx, dz):
        return lax.rem(x + dx + NX, NX), lax.rem(z + dz + NZ, NZ)

    def plane(x2, z2, c2):
        return ((x2 * NZ + z2) * 2 + c2, mu)

    def tensor_chunk(w):
        return pltpu.make_async_copy(tensor.at[pl.ds(w * YR, YR)], tb.at[lax.rem(w, 2)], t_sem.at[lax.rem(w, 2)])

    tensor_chunk(0).start()
    barrier = pltpu.get_barrier_semaphore()
    for c2 in (0, 1):
        for dx, dz in NEAR + [(0, 0)]:
            if (dx, dz, c2) != (0, 0, 0):
                pl.semaphore_signal(barrier, inc=1, device_id=plane(*moved(dx, dz), lax.rem(core + c2, 2)), device_id_type=MESH)
    for dy in DY:
        pl.semaphore_signal(barrier, inc=1, device_id=(pa, lax.rem(mu + dy, NY)), device_id_type=MESH)
    pl.semaphore_wait(barrier, 2 * CHIPS - 1 + NY - 1)

    def send_x(w, carry):
        def part(x2, z2, c2):
            return tensor.at[
                pl.ds(w * XR, XR),
                pl.ds(pl.multiple_of(mu * (NAO // NY) + x2 * 2 * LB + c2 * LB, LB), LB),
                pl.ds(pl.multiple_of(z2 * SB, SB), SB),
            ]

        for c2 in (0, 1):
            for dx, dz in NEAR + [(0, 0)]:
                where = (*moved(dx, dz), lax.rem(core + c2, 2))
                if (dx, dz, c2) == (0, 0, 0):
                    pltpu.make_async_copy(part(*where), xr.at[w, pa], x_recv.at[w]).start()
                else:
                    pltpu.make_async_remote_copy(
                        src_ref=part(*where), dst_ref=xr.at[w, pa], send_sem=x_send.at[w], recv_sem=x_recv.at[w],
                        device_id=plane(*where), device_id_type=MESH,
                    ).start()
        return carry

    lax.fori_loop(0, XW, send_x, 0)

    spread = (block_of((NAO, 8), 0) == lax.broadcasted_iota(jnp.int32, (NAO, 8), 1)).astype(F32)
    for g in range(3):
        blocks = mask[(ROWS * pa + 16 * g) // BS].astype(F32)
        rows = jnp.dot(spread, blocks, preferred_element_type=F32)
        me[g] = lax.dot_general(rows, spread, (((1,), (1,)), ((), ())), preferred_element_type=F32).astype(BF16)
    lane_block = lax.broadcasted_iota(jnp.int32, (8, SB), 0) == block_of((8, SB), 1, 2 * z)
    own_blocks = mask[:, pl.ds(2 * mu + x // 2, 1), :].astype(F32).reshape(NP // BS, 8)
    mv[...] = jnp.dot(own_blocks, lane_block.astype(F32), preferred_element_type=F32)
    group_row = group[...].astype(F32)
    row_group = jnp.sum(spread * group_row, axis=1, keepdims=True)
    col_group = lax.dot_general(group_row, spread, (((1,), (1,)), ((), ())), preferred_element_type=F32)
    vm[...] = jnp.where(jnp.abs(row_group - col_group) <= GROUP_REACH + 0.5, virt[...].astype(F32), 0.0).astype(BF16)
    occ_block = lax.broadcasted_iota(jnp.int32, (8, SB), 0) == block_of((8, SB), 1, 2 * mu)
    occ_group = jnp.dot(group_row, occ_block.astype(F32), preferred_element_type=F32)
    occ_cols = occ[:, pl.ds(pl.multiple_of(mu * SB, SB), SB)].astype(F32)
    occ_cols = jnp.where(jnp.abs(row_group - occ_group) <= GROUP_REACH + 0.5, occ_cols, 0.0)
    occ_t[...] = occ_cols.T.astype(BF16)
    to = lax.broadcasted_iota(jnp.int32, (256, 256), 0)
    perm[...] = (lax.broadcasted_iota(jnp.int32, (256, 256), 1) == lax.rem(to, 16) * 16 + to // 16).astype(BF16)

    def send_y(w):
        def part(x2, z2):
            return ys.at[pl.ds(w * YR, YR), pl.ds(pl.multiple_of(x2 * 2 * LB, 2 * LB), 2 * LB), pl.ds(pl.multiple_of(z2 * SB, SB), SB)]

        for dx, dz in NEAR:
            x2, z2 = moved(dx, dz)
            pltpu.make_async_remote_copy(
                src_ref=part(x2, z2), dst_ref=yr.at[w, chip], send_sem=y_send.at[w], recv_sem=y_recv.at[w],
                device_id=plane(x2, z2, core), device_id_type=MESH,
            ).start()
        pltpu.make_async_copy(part(x, z), yr.at[w, chip], y_recv.at[w]).start()

    def make_product(w, carry):
        tensor_chunk(w).wait()

        @pl.when(w + 1 < YW)
        def _():
            tensor_chunk(w + 1).start()

        slot = lax.rem(w, 2)

        def one(p, carry):
            block = tb[slot, p] * me[w // 2]
            half[pl.ds(pl.multiple_of(p * SB, SB), SB), :] = jnp.dot(occ_t[...], block, preferred_element_type=F32).astype(BF16)
            return carry

        lax.fori_loop(0, YR, one, 0)

        def two(i, carry):
            rows = half[pl.ds(pl.multiple_of(i * 2 * SB, 2 * SB), 2 * SB), :]
            done = jnp.dot(rows, vm[...], preferred_element_type=F32).astype(BF16)
            ys[pl.ds(w * YR + 2 * i, 2)] = done.reshape(2, SB, NAO)
            return carry

        lax.fori_loop(0, YR // 2, two, 0)
        send_y(w)
        return carry

    lax.fori_loop(0, YW, make_product, 0)

    def sibling(rows, columns):
        return pltpu.make_async_remote_copy(
            src_ref=xl.at[rows, columns], dst_ref=xl.at[rows, columns], send_sem=l_send, recv_sem=l_recv,
            device_id=plane(x, z, 1 - core), device_id_type=MESH,
        )

    own = pl.multiple_of(core * KC, KC)
    other = pl.multiple_of((1 - core) * KC, KC)

    def turn(rows):
        return jnp.dot(perm[...], rows, preferred_element_type=F32).astype(BF16).reshape(16, 16, SB)

    def lay_x(w, carry):
        pltpu.make_async_copy(xr.at[w], xr.at[w], x_recv.at[w]).wait()

        def one(j, carry):
            row = pl.multiple_of(j * ROWS + w * XR, XR)
            keep = mv[pl.ds(row // BS, 1), :].astype(BF16)
            turned = turn(xr[w, j].reshape(256, SB) * keep)
            for i in range(LB):
                xl[pl.ds(row, XR), pl.ds(pl.multiple_of(own + i * SB, SB), SB)] = turned[i]
            sibling(pl.ds(row, XR), pl.ds(own, KC)).start()
            return carry

        lax.fori_loop(0, 2 * CHIPS, one, 0)
        return carry

    lax.fori_loop(0, XW, lay_x, 0)
    pltpu.make_async_copy(xl.at[:, pl.ds(other, KC)], xl.at[:, pl.ds(other, KC)], l_recv).wait()

    def partial(w, carry):
        pltpu.make_async_copy(yr.at[w], yr.at[w], y_recv.at[w]).wait()

        def lay_y(i, carry):
            for h in (0, 1):
                turned = turn(yr[w, pl.ds(2 * i, 2), :, h * LB : (h + 1) * LB, :].reshape(256, SB))
                for k in range(LB):
                    yl[pl.ds(pl.multiple_of(i * 16, 16), 16), (h * LB + k) * SB : (h * LB + k + 1) * SB] = turned[k]
            return carry

        lax.fori_loop(0, CHIPS // 2, lay_y, 0)

        def tile(y2):
            columns = xl[pl.ds(pl.multiple_of(y2 * QC, QC), QC), :]
            return lax.dot_general(yl[...], columns, (((1,), (1,)), ((), ())), preferred_element_type=F32)

        for k, dy in enumerate(DY):
            y2 = lax.rem(mu + dy, NY)
            cb[w, k] = tile(y2)
            pltpu.make_async_remote_copy(
                src_ref=cb.at[w, k], dst_ref=yrs.at[w, k], send_sem=c_send.at[w], recv_sem=c_recv.at[w],
                device_id=(pa, y2), device_id_type=MESH,
            ).start()
        sb[w] = tile(mu)

        @pl.when(w > 0)
        def _():
            sum_y(w - 1)

        return carry

    def sum_y(w):
        pltpu.make_async_copy(yrs.at[w], yrs.at[w], c_recv.at[w]).wait()
        sb[w] = (sb[w] + yrs[w, 0]) + (yrs[w, 1] + yrs[w, 2])

        def part(there):
            return sb.at[w, pl.ds(pl.multiple_of(there * YR, YR), YR)]

        for dx, dz in NEAR:
            x2, z2 = moved(dx, dz)
            pltpu.make_async_remote_copy(
                src_ref=part(x2 * NZ + z2), dst_ref=zr.at[w, chip], send_sem=z_send.at[w], recv_sem=z_recv.at[w],
                device_id=plane(x2, z2, core), device_id_type=MESH,
            ).start()
        pltpu.make_async_copy(part(chip), zr.at[w, chip], z_recv.at[w]).start()

    lax.fori_loop(0, YW, partial, 0)
    sum_y(YW - 1)

    def finish(w, carry):
        pltpu.make_async_copy(zr.at[w], zr.at[w], z_recv.at[w]).wait()
        out[pl.ds(pl.multiple_of(w * YR, YR), YR), :] = jnp.sum(zr[w], axis=0) * (1.0 / NAO)
        return carry

    lax.fori_loop(0, YW, finish, 0)

    def left(ref, sem):
        pltpu.make_async_copy(ref, ref, sem).wait()

    left(xl.at[:, pl.ds(own, KC)], l_send)
    for w in range(XW):
        left(xr.at[w, pl.ds(0, 2 * CHIPS - 1)], x_send.at[w])
    for w in range(YW):
        left(yr.at[w, pl.ds(0, CHIPS - 1)], y_send.at[w])
        left(cb.at[w], c_send.at[w])
        left(zr.at[w, pl.ds(0, CHIPS - 1)], z_send.at[w])


def shards(tensor, block_mask, group_of_block, green_occ, green_virt):
    vmem = pl.BlockSpec(memory_space=pltpu.VMEM)
    dma = pltpu.SemaphoreType.DMA
    return pl.pallas_call(
        kernel,
        out_shape=jax.ShapeDtypeStruct((ROWS, QC), F32),
        in_specs=[pl.BlockSpec(memory_space=pl.ANY), vmem, vmem, vmem, vmem],
        out_specs=vmem,
        scratch_shapes=[
            pltpu.VMEM((XW, 2 * CHIPS, XR, LB, SB), BF16),
            pltpu.VMEM((NP, 2 * KC), BF16),
            pltpu.VMEM((2, YR, NAO, NAO), BF16),
            pltpu.VMEM((3, NAO, NAO), BF16),
            pltpu.VMEM((SB, NAO), BF16),
            pltpu.VMEM((NAO, NAO), BF16),
            pltpu.VMEM((NP // BS, SB), F32),
            pltpu.VMEM((256, 256), BF16),
            pltpu.VMEM((YR * SB, NAO), BF16),
            pltpu.VMEM((ROWS, SB, NAO), BF16),
            pltpu.VMEM((YW, CHIPS, YR, 2 * LB, SB), BF16),
            pltpu.VMEM((WR, 2 * KC), BF16),
            pltpu.VMEM((YW, NY - 1, WR, QC), F32),
            pltpu.VMEM((YW, WR, QC), F32),
            pltpu.VMEM((YW, NY - 1, WR, QC), F32),
            pltpu.VMEM((YW, CHIPS, YR, QC), F32),
            dma((XW,)), dma((XW,)), dma, dma, dma((2,)), dma((YW,)), dma((YW,)), dma((YW,)), dma((YW,)), dma((YW,)), dma((YW,)),
        ],
        compiler_params=pltpu.CompilerParams(collective_id=0, has_side_effects=True, vmem_limit_bytes=60 * 2**20),
    )(tensor, block_mask, group_of_block.reshape(1, 8), green_occ, green_virt)


def solution(mesh):
    placed = (P("pa", None, None), P(), P(), P(), P())
    return jax.shard_map(shards, mesh=mesh, in_specs=placed, out_specs=P("pa", "mu"), check_vma=False)
```

time: 381 us -> 179 us (0.47)
  Pallas kernels: 0 us -> 175 us
  waiting for transfers between devices: 171 us -> 0 us
  blocking collectives: 85.6 us -> 0 us
  local copies, waits for them, and re-layouts: 47.2 us -> 2.99 us
  matrix products: 34 us -> 0 us
  other arithmetic: 20.9 us -> 0 us
  between operations: 13.5 us -> 0.01 us
  starting transfers between devices: 8.45 us -> 0 us
    pallas_call x0 -> x1, Pallas kernels: none -> 175 us  [shards(): pl.pallas_call(kernel, out_shape=jax.ShapeDtypeStruct((ROWS, QC), F32), i...]
    reduce_scatter x2 -> x0, waiting for transfers between devices: 116 us -> none  [the longest x1 93.9 us: shards(): row_part = lax.psum_scatter(term, 'pa', scatter_dimension=0, tiled=True)]
    all_to_all x1 -> x0, blocking collectives: 85.6 us -> none  [shards(): lax.all_to_all(own_rows, 'pa', split_axis=1, concat_axis=0, tiled=True)]
    all_to_all x1 -> x0, waiting for transfers between devices: 54.1 us -> none  [shards(): lax.all_to_all(product, 'pa', split_axis=1, concat_axis=0, tiled=True)]
    all_to_all x4 -> x0, local copies, waits for them, and re-layouts: 39.2 us -> none  [the longest x2 19.7 us: shards(): lax.all_to_all(product, 'pa', split_axis=1, concat_axis=0, tiled=True)]
    dot_general x3 -> x0, matrix products: 34 us -> none  [the longest x1 19.4 us: shards(): jnp.einsum('pln,ns->pls', half, virt, preferred_element_type=jnp.float32)]
    mul x1 -> x0, other arithmetic: 20.6 us -> none  [shards(): tensor.reshape(p_rows, nab, BS, nao) * expanded[:, :, None, :]]
    all_to_all x1 -> x0, starting transfers between devices: 8.36 us -> none  [shards(): lax.all_to_all(product, 'pa', split_axis=1, concat_axis=0, tiled=True)]
  transfers between devices with their start and end apart: 3 -> 0, of which waited for: 3 -> 0; matrix products, arithmetic and copies ran while one was open for 4% -> 0% of each run, Pallas kernels for 0% -> 0%
where the time goes in v1:
time: 179 us; the launch traced here: 178 us
  Pallas kernels  175 us (98%)
  local copies, waits for them, and re-layouts  2.99 us (2%)
    pallas_call x1, Pallas kernels, shards(): pl.pallas_call(kernel, out_shape=jax.ShapeDtypeStruct((ROWS, QC), F32), i...  175 us

profile of v1, /device:TPU:0, one launch (start us, length us, event | category | flops | bytes accessed | tf_op | source)
XLA Modules:
  0.0 178.5 jit_solution(16291022399351489438)
XLA Ops:
  0.0 1.5 copy.6.mask
  1.5 175.5 %shard_map.55 = f32[48,384]{1,0:T(8,128)} custom-call(bf16[48,512,512]{2,1,0:T(8,128)(2,1)} %tensor.1, s32[24,8,8]{2,1,0:T(8,128)} %copy.6.mask, s32[1,8]{1,0:T(1,128)} %bitcast.1, bf16[512,512]{1,0:T(8,128)(2,1)} %occ.1, bf16[512,512]{1,0:T(8,128)(2,1)} %virt.1), custom_call_target="tpu_custom_call" | custom-call | tf_op jit(solution)/shard_map/pallas_call | solution.py:246
  177.0 1.5 copy.8

commit v2 on v1

--- a/solution.py
+++ b/solution.py
@@ -22,6 +22,10 @@
 XR = ROWS // XW
 YW = 6
 YR = ROWS // YW
+TR = 8
+ZW = 3
+ZR = ROWS // ZW
+YZ = ZR // YR
 WR = CHIPS * YR
 QC = NP // NY
 NEAR = [(1, 0), (0, 1), (-1, 0), (0, -1), (1, 1), (-1, -1), (1, -1), (-1, 1), (2, 0), (0, 2), (2, 1), (1, 2), (2, -1), (-1, 2), (2, 2)]
@@ -34,7 +38,7 @@
 
 def kernel(
     tensor, mask, group, occ, virt, out,
-    xr, xl, tb, me, occ_t, vm, mv, perm, half, ys, yr, yl, cb, sb, yrs, zr,
+    xr, xl, tb, me, occ_t, vm, mv, perm, half, ys, yr, yl, cb, sb, yrs, zf, zb, zr,
     x_send, x_recv, l_send, l_recv, t_sem, y_send, y_recv, c_send, c_recv, z_send, z_recv,
 ):
     pa, mu = lax.axis_index("pa"), lax.axis_index("mu")
@@ -42,13 +46,13 @@
     chip = x * NZ + z
 
     def moved(dx, dz):
-        return lax.rem(x + dx + NX, NX), lax.rem(z + dz + NZ, NZ)
+        return lax.rem(x + dx + core * (dz - dx) + NX, NX), lax.rem(z + dz + core * (dx - dz) + NZ, NZ)
 
     def plane(x2, z2, c2):
         return ((x2 * NZ + z2) * 2 + c2, mu)
 
     def tensor_chunk(w):
-        return pltpu.make_async_copy(tensor.at[pl.ds(w * YR, YR)], tb.at[lax.rem(w, 2)], t_sem.at[lax.rem(w, 2)])
+        return pltpu.make_async_copy(tensor.at[pl.ds(w * TR, TR)], tb.at[lax.rem(w, 2)], t_sem.at[lax.rem(w, 2)])
 
     tensor_chunk(0).start()
     barrier = pltpu.get_barrier_semaphore()
@@ -117,7 +121,7 @@
     def make_product(w, carry):
         tensor_chunk(w).wait()
 
-        @pl.when(w + 1 < YW)
+        @pl.when(w + 1 < ROWS // TR)
         def _():
             tensor_chunk(w + 1).start()
 
@@ -128,19 +132,20 @@
             half[pl.ds(pl.multiple_of(p * SB, SB), SB), :] = jnp.dot(occ_t[...], block, preferred_element_type=F32).astype(BF16)
             return carry
 
-        lax.fori_loop(0, YR, one, 0)
+        lax.fori_loop(0, TR, one, 0)
 
         def two(i, carry):
             rows = half[pl.ds(pl.multiple_of(i * 2 * SB, 2 * SB), 2 * SB), :]
             done = jnp.dot(rows, vm[...], preferred_element_type=F32).astype(BF16)
-            ys[pl.ds(w * YR + 2 * i, 2)] = done.reshape(2, SB, NAO)
-            return carry
-
-        lax.fori_loop(0, YR // 2, two, 0)
-        send_y(w)
-        return carry
-
-    lax.fori_loop(0, YW, make_product, 0)
+            ys[pl.ds(w * TR + 2 * i, 2)] = done.reshape(2, SB, NAO)
+            return carry
+
+        lax.fori_loop(0, TR // 2, two, 0)
+        for k in range(TR // YR):
+            send_y(w * (TR // YR) + k)
+        return carry
+
+    lax.fori_loop(0, ROWS // TR, make_product, 0)
 
     def sibling(rows, columns):
         return pltpu.make_async_remote_copy(
@@ -177,12 +182,12 @@
 
         def lay_y(i, carry):
             for h in (0, 1):
-                turned = turn(yr[w, pl.ds(2 * i, 2), :, h * LB : (h + 1) * LB, :].reshape(256, SB))
+                turned = turn(yr[w, pl.ds(16 // YR * i, 16 // YR), :, h * LB : (h + 1) * LB, :].reshape(256, SB))
                 for k in range(LB):
                     yl[pl.ds(pl.multiple_of(i * 16, 16), 16), (h * LB + k) * SB : (h * LB + k + 1) * SB] = turned[k]
             return carry
 
-        lax.fori_loop(0, CHIPS // 2, lay_y, 0)
+        lax.fori_loop(0, WR // 16, lay_y, 0)
 
         def tile(y2):
             columns = xl[pl.ds(pl.multiple_of(y2 * QC, QC), QC), :]
@@ -190,12 +195,12 @@
 
         for k, dy in enumerate(DY):
             y2 = lax.rem(mu + dy, NY)
-            cb[w, k] = tile(y2)
+            cb[w, k] = tile(y2).astype(BF16)
             pltpu.make_async_remote_copy(
                 src_ref=cb.at[w, k], dst_ref=yrs.at[w, k], send_sem=c_send.at[w], recv_sem=c_recv.at[w],
                 device_id=(pa, y2), device_id_type=MESH,
             ).start()
-        sb[w] = tile(mu)
+        sb[lax.rem(w, 2)] = tile(mu)
 
         @pl.when(w > 0)
         def _():
@@ -205,28 +210,36 @@
 
     def sum_y(w):
         pltpu.make_async_copy(yrs.at[w], yrs.at[w], c_recv.at[w]).wait()
-        sb[w] = (sb[w] + yrs[w, 0]) + (yrs[w, 1] + yrs[w, 2])
-
-        def part(there):
-            return sb.at[w, pl.ds(pl.multiple_of(there * YR, YR), YR)]
-
+        total = (sb[lax.rem(w, 2)] + yrs[w, 0].astype(F32)) + (yrs[w, 1].astype(F32) + yrs[w, 2].astype(F32))
+        for k in range(YZ):
+
+            @pl.when(lax.rem(w, YZ) == k)
+            def _():
+                zf[:, k * YR : (k + 1) * YR, :] = total.reshape(CHIPS, YR, QC)
+
+        @pl.when(lax.rem(w, YZ) == YZ - 1)
+        def _():
+            send_z(w // YZ)
+
+    def send_z(v):
+        zb[v] = zf[...].astype(BF16)
         for dx, dz in NEAR:
             x2, z2 = moved(dx, dz)
             pltpu.make_async_remote_copy(
-                src_ref=part(x2 * NZ + z2), dst_ref=zr.at[w, chip], send_sem=z_send.at[w], recv_sem=z_recv.at[w],
+                src_ref=zb.at[v, x2 * NZ + z2], dst_ref=zr.at[v, chip], send_sem=z_send.at[v], recv_sem=z_recv.at[v],
                 device_id=plane(x2, z2, core), device_id_type=MESH,
             ).start()
-        pltpu.make_async_copy(part(chip), zr.at[w, chip], z_recv.at[w]).start()
+        pltpu.make_async_copy(zb.at[v, chip], zr.at[v, chip], z_recv.at[v]).start()
 
     lax.fori_loop(0, YW, partial, 0)
     sum_y(YW - 1)
 
     def finish(w, carry):
         pltpu.make_async_copy(zr.at[w], zr.at[w], z_recv.at[w]).wait()
-        out[pl.ds(pl.multiple_of(w * YR, YR), YR), :] = jnp.sum(zr[w], axis=0) * (1.0 / NAO)
-        return carry
-
-    lax.fori_loop(0, YW, finish, 0)
+        out[pl.ds(pl.multiple_of(w * ZR, ZR), ZR), :] = jnp.sum(zr[w].astype(F32), axis=0) * (1.0 / NAO)
+        return carry
+
+    lax.fori_loop(0, ZW, finish, 0)
 
     def left(ref, sem):
         pltpu.make_async_copy(ref, ref, sem).wait()
@@ -237,6 +250,7 @@
     for w in range(YW):
         left(yr.at[w, pl.ds(0, CHIPS - 1)], y_send.at[w])
         left(cb.at[w], c_send.at[w])
+    for w in range(ZW):
         left(zr.at[w, pl.ds(0, CHIPS - 1)], z_send.at[w])
 
 
@@ -251,21 +265,23 @@
         scratch_shapes=[
             pltpu.VMEM((XW, 2 * CHIPS, XR, LB, SB), BF16),
             pltpu.VMEM((NP, 2 * KC), BF16),
-            pltpu.VMEM((2, YR, NAO, NAO), BF16),
+            pltpu.VMEM((2, TR, NAO, NAO), BF16),
             pltpu.VMEM((3, NAO, NAO), BF16),
             pltpu.VMEM((SB, NAO), BF16),
             pltpu.VMEM((NAO, NAO), BF16),
             pltpu.VMEM((NP // BS, SB), F32),
             pltpu.VMEM((256, 256), BF16),
-            pltpu.VMEM((YR * SB, NAO), BF16),
+            pltpu.VMEM((TR * SB, NAO), BF16),
             pltpu.VMEM((ROWS, SB, NAO), BF16),
             pltpu.VMEM((YW, CHIPS, YR, 2 * LB, SB), BF16),
             pltpu.VMEM((WR, 2 * KC), BF16),
-            pltpu.VMEM((YW, NY - 1, WR, QC), F32),
-            pltpu.VMEM((YW, WR, QC), F32),
-            pltpu.VMEM((YW, NY - 1, WR, QC), F32),
-            pltpu.VMEM((YW, CHIPS, YR, QC), F32),
-            dma((XW,)), dma((XW,)), dma, dma, dma((2,)), dma((YW,)), dma((YW,)), dma((YW,)), dma((YW,)), dma((YW,)), dma((YW,)),
+            pltpu.VMEM((YW, NY - 1, WR, QC), BF16),
+            pltpu.VMEM((2, WR, QC), F32),
+            pltpu.VMEM((YW, NY - 1, WR, QC), BF16),
+            pltpu.VMEM((CHIPS, ZR, QC), F32),
+            pltpu.VMEM((ZW, CHIPS, ZR, QC), BF16),
+            pltpu.VMEM((ZW, CHIPS, ZR, QC), BF16),
+            dma((XW,)), dma((XW,)), dma, dma, dma((2,)), dma((YW,)), dma((YW,)), dma((YW,)), dma((YW,)), dma((ZW,)), dma((ZW,)),
         ],
         compiler_params=pltpu.CompilerParams(collective_id=0, has_side_effects=True, vmem_limit_bytes=60 * 2**20),
     )(tensor, block_mask, group_of_block.reshape(1, 8), green_occ, green_virt)

time: 179 us -> 169 us (0.944)
  Pallas kernels: 175 us -> 165 us
    pallas_call x1, Pallas kernels: 175 us -> 165 us  [shards(): pl.pallas_call(kernel, out_shape=jax.ShapeDtypeStruct((ROWS, QC), F32), i...]
where the time goes in v2:
time: 169 us; the launch traced here: 168 us
  Pallas kernels  165 us (98%)
  local copies, waits for them, and re-layouts  2.99 us (2%)
    pallas_call x1, Pallas kernels, shards(): pl.pallas_call(kernel, out_shape=jax.ShapeDtypeStruct((ROWS, QC), F32), i...  165 us

profile of v2, /device:TPU:0, one launch (start us, length us, event | category | flops | bytes accessed | tf_op | source)
XLA Modules:
  0.0 168.5 jit_solution(14613246225943938845)
XLA Ops:
  0.0 1.5 copy.6.mask
  1.5 165.5 %shard_map.55 = f32[48,384]{1,0:T(8,128)} custom-call(bf16[48,512,512]{2,1,0:T(8,128)(2,1)} %tensor.1, s32[24,8,8]{2,1,0:T(8,128)} %copy.6.mask, s32[1,8]{1,0:T(1,128)} %bitcast.1, bf16[512,512]{1,0:T(8,128)(2,1)} %occ.1, bf16[512,512]{1,0:T(8,128)(2,1)} %virt.1), custom_call_target="tpu_custom_call" | custom-call | tf_op jit(solution)/shard_map/pallas_call | solution.py:260
  167.0 1.5 copy.8

commit v3 on v2

--- a/solution.py
+++ b/solution.py
@@ -32,6 +32,12 @@
 DY = (2, 1, 3)
 
 
+SLOTS = 60
+PW = 4
+UNITS = 3 * 64
+SR = 4
+
+
 def block_of(shape, dim, first=0):
     return lax.broadcasted_iota(jnp.int32, shape, dim) // BS + first
 
@@ -254,7 +260,7 @@
         left(zr.at[w, pl.ds(0, CHIPS - 1)], z_send.at[w])
 
 
-def shards(tensor, block_mask, group_of_block, green_occ, green_virt):
+def whole(tensor, block_mask, group_row, green_occ, green_virt):
     vmem = pl.BlockSpec(memory_space=pltpu.VMEM)
     dma = pltpu.SemaphoreType.DMA
     return pl.pallas_call(
@@ -284,7 +290,294 @@
             dma((XW,)), dma((XW,)), dma, dma, dma((2,)), dma((YW,)), dma((YW,)), dma((YW,)), dma((YW,)), dma((ZW,)), dma((ZW,)),
         ],
         compiler_params=pltpu.CompilerParams(collective_id=0, has_side_effects=True, vmem_limit_bytes=60 * 2**20),
-    )(tensor, block_mask, group_of_block.reshape(1, 8), green_occ, green_virt)
+    )(tensor, block_mask, group_row, green_occ, green_virt)
+
+
+def dot(a, b):
+    return jnp.dot(a, b, preferred_element_type=F32)
+
+
+def iota(shape, dim):
+    return lax.broadcasted_iota(jnp.int32, shape, dim)
+
+
+def packed_kernel(
+    tensor, mask, group, occ, virt, out,
+    xin, xs, xr, xl, tb, me, occ_f, occ_t, vm, perms, sel, tabs, own_pos, half, ys, yr, yl, cb, sb, yrs, zf, zb, zr, spots,
+    i_sem, x_send, x_recv, l_send, l_recv, t_sem, y_send, y_recv, c_send, c_recv, z_send, z_recv, s_sem,
+):
+    pa, mu = lax.axis_index("pa"), lax.axis_index("mu")
+    x, z, core = pa // (2 * NZ), lax.rem(pa // 2, NZ), lax.rem(pa, 2)
+    chip = x * NZ + z
+
+    def moved(dx, dz):
+        return lax.rem(x + dx + core * (dz - dx) + NX, NX), lax.rem(z + dz + core * (dx - dz) + NZ, NZ)
+
+    def plane(x2, z2, c2):
+        return ((x2 * NZ + z2) * 2 + c2, mu)
+
+    def wait(ref, sem):
+        pltpu.make_async_copy(ref, ref, sem).wait()
+
+    def to_chips(source, target, send, recv):
+        for dx, dz in NEAR:
+            x2, z2 = moved(dx, dz)
+            pltpu.make_async_remote_copy(
+                src_ref=source(x2 * NZ + z2), dst_ref=target, send_sem=send, recv_sem=recv,
+                device_id=plane(x2, z2, core), device_id_type=MESH,
+            ).start()
+        pltpu.make_async_copy(source(chip), target, recv).start()
+
+    def tensor_chunk(w):
+        return pltpu.make_async_copy(tensor.at[pl.ds(w * SR, SR)], tb.at[lax.rem(w, 2)], t_sem.at[lax.rem(w, 2)])
+
+    def load_x(u, carry):
+        g, a, b = u // 32, lax.rem(u // 4, 8), lax.rem(u, 4)
+        pltpu.make_async_copy(
+            tensor.at[pl.ds(g * 16, 16), pl.ds(pl.multiple_of(a * BS + mu * LB, LB), LB), pl.ds(pl.multiple_of(b * SB, SB), SB)],
+            xin.at[u], i_sem,
+        ).start()
+        return carry
+
+    lax.fori_loop(0, UNITS // 2, load_x, 0)
+    tensor_chunk(0).start()
+    barrier = pltpu.get_barrier_semaphore()
+    for dx, dz in NEAR:
+        pl.semaphore_signal(barrier, inc=1, device_id=plane(*moved(dx, dz), core), device_id_type=MESH)
+    pl.semaphore_signal(barrier, inc=1, device_id=plane(x, z, 1 - core), device_id_type=MESH)
+    for dy in DY:
+        pl.semaphore_signal(barrier, inc=1, device_id=(pa, lax.rem(mu + dy, NY)), device_id_type=MESH)
+
+    flat = jnp.zeros((NP // BS, 64), F32)
+    for a in range(8):
+        place = (iota((8, 64), 1) == iota((8, 64), 0) + 8 * a).astype(F32)
+        flat += dot(mask[:, a, :].astype(F32), place)
+    kept = jnp.zeros((2 * CHIPS, 256), F32)
+    for g in range(3):
+        rows = ((iota((2 * CHIPS, NP // BS), 0) * ROWS + 16 * g) // BS == iota((2 * CHIPS, NP // BS), 1)).astype(F32)
+        place = (iota((64, 256), 1) == iota((64, 256), 0) + 64 * g).astype(F32)
+        kept += dot(dot(rows, flat), place)
+    upto = (iota((256, 256), 0) <= iota((256, 256), 1)).astype(F32)
+    place_of = dot(kept, upto)
+    own_pos[...] = place_of * kept
+    order = place_of.astype(jnp.int32) - 1
+    odd = lax.rem(iota((2 * CHIPS, 256), 1), 2)
+    spot = order // 2 + jnp.where(lax.rem(order + 2, 2) == odd, 0, SLOTS)
+    tabs[0 : 2 * CHIPS] = jnp.clip(jnp.where(kept > 0.5, spot, 2 * SLOTS), 0, 2 * SLOTS)
+    taken = (own_pos[pl.ds(pa, 1), :] == (iota((256, 256), 0) + 1).astype(F32)).astype(F32)
+    units = iota((8, 256), 1).astype(F32)
+    unit = lax.dot_general(units, taken, (((1,), (1,)), ((), ())), preferred_element_type=F32).astype(jnp.int32)
+    there = lax.dot_general(jnp.ones((8, 256), F32), taken, (((1,), (1,)), ((), ())), preferred_element_type=F32).astype(jnp.int32)
+    tabs[2 * CHIPS : 2 * CHIPS + 8] = jnp.clip(unit // 2, 0, UNITS // 2 - 1)
+    tabs[2 * CHIPS + 8 : 2 * CHIPS + 16] = jnp.clip(there * (1 + lax.rem(unit, 2)), 0, 2)
+    to_smem = pltpu.make_async_copy(tabs, spots, s_sem)
+    to_smem.start()
+
+    to, at = iota((256, 256), 0), iota((256, 256), 1)
+    perms[0] = (at == lax.rem(to, 16) * 16 + to // 16).astype(BF16)
+    perms[1] = (at == (lax.rem(to, 8) * 2 + lax.rem(to // 8, 2)) * 16 + to // 16).astype(BF16)
+    perms[2] = (at == lax.rem(to, 128) // 8 * 16 + to // 128 * 8 + lax.rem(to, 8)).astype(BF16)
+    frm, into = iota((SB, SB), 0), iota((SB, SB), 1)
+    for h in (0, 1):
+        sel[0, h] = jnp.zeros((SB, SB), BF16)
+        for b in (0, 1):
+            sel[1 + b, h] = ((frm - BS * b == into - BS * h) & (into // BS == h)).astype(BF16)
+    sel[3, 0] = (lax.rem(frm + BS, SB) == into).astype(BF16)
+
+    to_smem.wait()
+    wait(xin, i_sem)
+    pl.semaphore_wait(barrier, CHIPS + NY - 1)
+
+    def pack(w, carry):
+        def one(i, carry):
+            for k in range(3):
+                r = w * (SLOTS // PW) + i * 3 + k
+                full = jnp.zeros((256, SB), F32)
+                for h in (0, 1):
+                    cube = xin[spots[2 * CHIPS, 2 * r + h]].reshape(256, SB)
+                    full += dot(cube, sel[spots[2 * CHIPS + 8, 2 * r + h], h])
+                xs[:, r] = dot(perms[0], full.astype(BF16)).astype(BF16).reshape(16, 16, SB)
+            return carry
+
+        lax.fori_loop(0, SLOTS // PW // 3, one, 0)
+        slots = pl.ds(w * (SLOTS // PW), SLOTS // PW)
+        to_chips(lambda t: xs.at[t, slots], xr.at[chip, slots], x_send.at[w], x_recv.at[w])
+        return carry
+
+    lax.fori_loop(0, PW, pack, 0)
+
+    spread = (block_of((NAO, 8), 0) == iota((NAO, 8), 1)).astype(F32)
+    for g in range(3):
+        rows = dot(spread, mask[(ROWS * pa + 16 * g) // BS].astype(F32))
+        me[g] = lax.dot_general(rows, spread, (((1,), (1,)), ((), ())), preferred_element_type=F32).astype(BF16)
+    group_row = group[...].astype(F32)
+    row_group = jnp.sum(spread * group_row, axis=1, keepdims=True)
+    col_group = lax.dot_general(group_row, spread, (((1,), (1,)), ((), ())), preferred_element_type=F32)
+    near = jnp.abs(row_group - col_group) <= GROUP_REACH + 0.5
+    vm[...] = jnp.where(near, virt[...].astype(F32), 0.0).astype(BF16)
+    occ_f[...] = jnp.where(near, occ[...].astype(F32), 0.0).T
+    for a in range(8):
+        occ_t[a * LB : (a + 1) * LB] = occ_f[pl.ds(pl.multiple_of(a * BS + mu * LB, LB), LB), :].astype(BF16)
+
+    def make_product(w, carry):
+        for part in range(YR // SR):
+            v = w * (YR // SR) + part
+            tensor_chunk(v).wait()
+
+            @pl.when(v + 1 < ROWS // SR)
+            def _():
+                tensor_chunk(v + 1).start()
+
+            def one(p, carry):
+                block = tb[lax.rem(v, 2), p] * me[w // 2]
+                half[part * SR + p] = dot(occ_t[...], block).astype(BF16)
+                return carry
+
+            lax.fori_loop(0, SR, one, 0)
+        for a in range(4):
+            done = dot(half[:, a * 2 * LB : (a + 1) * 2 * LB, :].reshape(256, NAO), vm[...]).astype(BF16)
+            ys[w, :, :, a * NAO : (a + 1) * NAO] = dot(perms[1], done).astype(BF16).reshape(16, 16, NAO)
+        to_chips(lambda t: ys.at[w, t], yr.at[w, chip], y_send.at[w], y_recv.at[w])
+        return carry
+
+    lax.fori_loop(0, YW, make_product, 0)
+
+    for w in range(PW):
+        slots = pl.ds(w * (SLOTS // PW), SLOTS // PW)
+        wait(xr.at[:, slots], x_recv.at[w])
+    left_half = iota((16, SB), 1) < BS
+
+    def unpack(i, carry):
+        rows = dot(xr[i, 0:SLOTS].reshape(SLOTS * 16, SB), sel[3, 0])
+        xr[i, SLOTS : 2 * SLOTS] = rows.astype(BF16).reshape(SLOTS, 16, SB)
+        xr[i, 2 * SLOTS] = jnp.zeros((16, SB), BF16)
+        j = 2 * i + core
+        for g in range(3):
+            row = pl.multiple_of(j * ROWS + g * 16, 16)
+            for a in range(8):
+                for b in range(4):
+                    u = (g * 8 + a) * 8 + 2 * b
+                    both = jnp.where(left_half, xr[i, spots[j, u]], xr[i, spots[j, u + 1]])
+                    first = a % 2 * KC + a // 2 * NAO + b * SB
+                    xl[pl.ds(row, 16), first : first + SB] = both
+        rows = pl.ds(pl.multiple_of(j * ROWS, 16), ROWS)
+        pltpu.make_async_remote_copy(
+            src_ref=xl.at[rows], dst_ref=xl.at[rows], send_sem=l_send, recv_sem=l_recv,
+            device_id=plane(x, z, 1 - core), device_id_type=MESH,
+        ).start()
+        return carry
+
+    lax.fori_loop(0, CHIPS, unpack, 0)
+    wait(xl.at[pl.ds(0, NP // 2)], l_recv)
+
+    def partial(w, carry):
+        wait(yr.at[w], y_recv.at[w])
+        for k in range(4):
+            rows = yr[w, :, :, k * NAO : (k + 1) * NAO].reshape(256, NAO)
+            turned = dot(perms[2], rows).astype(BF16)
+            yl[:, k * NAO : (k + 1) * NAO] = turned[:WR]
+            yl[:, KC + k * NAO : KC + (k + 1) * NAO] = turned[WR:]
+
+        def tile(y2):
+            columns = xl[pl.ds(pl.multiple_of(y2 * QC, QC), QC), :]
+            return lax.dot_general(yl[...], columns, (((1,), (1,)), ((), ())), preferred_element_type=F32)
+
+        for k, dy in enumerate(DY):
+            y2 = lax.rem(mu + dy, NY)
+            cb[w, k] = tile(y2).astype(BF16)
+            pltpu.make_async_remote_copy(
+                src_ref=cb.at[w, k], dst_ref=yrs.at[w, k], send_sem=c_send.at[w], recv_sem=c_recv.at[w],
+                device_id=(pa, y2), device_id_type=MESH,
+            ).start()
+        sb[lax.rem(w, 2)] = tile(mu)
+
+        @pl.when(w > 0)
+        def _():
+            sum_y(w - 1)
+
+        return carry
+
+    def sum_y(w):
+        wait(yrs.at[w], c_recv.at[w])
+        total = (sb[lax.rem(w, 2)] + yrs[w, 0].astype(F32)) + (yrs[w, 1].astype(F32) + yrs[w, 2].astype(F32))
+        for k in range(YZ):
+
+            @pl.when(lax.rem(w, YZ) == k)
+            def _():
+                zf[:, k * YR : (k + 1) * YR, :] = total.reshape(CHIPS, YR, QC)
+
+        @pl.when(lax.rem(w, YZ) == YZ - 1)
+        def _():
+            v = w // YZ
+            zb[v] = zf[...].astype(BF16)
+            to_chips(lambda t: zb.at[v, t], zr.at[v, chip], z_send.at[v], z_recv.at[v])
+
+    lax.fori_loop(0, YW, partial, 0)
+    sum_y(YW - 1)
+
+    def finish(w, carry):
+        wait(zr.at[w], z_recv.at[w])
+        out[pl.ds(pl.multiple_of(w * ZR, ZR), ZR), :] = jnp.sum(zr[w].astype(F32), axis=0) * (1.0 / NAO)
+        return carry
+
+    lax.fori_loop(0, ZW, finish, 0)
+
+    wait(xl.at[pl.ds(0, NP // 2)], l_send)
+    for w in range(PW):
+        wait(xs.at[pl.ds(0, CHIPS - 1), pl.ds(0, SLOTS // PW)], x_send.at[w])
+    for w in range(YW):
+        wait(yr.at[w, pl.ds(0, CHIPS - 1)], y_send.at[w])
+        wait(cb.at[w], c_send.at[w])
+    for w in range(ZW):
+        wait(zr.at[w, pl.ds(0, CHIPS - 1)], z_send.at[w])
+
+
+def packed(tensor, block_mask, group_row, green_occ, green_virt):
+    vmem = pl.BlockSpec(memory_space=pltpu.VMEM)
+    dma = pltpu.SemaphoreType.DMA
+    return pl.pallas_call(
+        packed_kernel,
+        out_shape=jax.ShapeDtypeStruct((ROWS, QC), F32),
+        in_specs=[pl.BlockSpec(memory_space=pl.ANY), vmem, vmem, vmem, vmem],
+        out_specs=vmem,
+        scratch_shapes=[
+            pltpu.VMEM((UNITS // 2, 16, LB, SB), BF16),
+            pltpu.VMEM((CHIPS, SLOTS, 16, SB), BF16),
+            pltpu.VMEM((CHIPS, 2 * SLOTS + 1, 16, SB), BF16),
+            pltpu.VMEM((NP, 2 * KC), BF16),
+            pltpu.VMEM((2, SR, NAO, NAO), BF16),
+            pltpu.VMEM((3, NAO, NAO), BF16),
+            pltpu.VMEM((NAO, NAO), F32),
+            pltpu.VMEM((SB, NAO), BF16),
+            pltpu.VMEM((NAO, NAO), BF16),
+            pltpu.VMEM((3, 256, 256), BF16),
+            pltpu.VMEM((4, 2, SB, SB), BF16),
+            pltpu.VMEM((2 * CHIPS + 16, 256), jnp.int32),
+            pltpu.VMEM((2 * CHIPS, 256), F32),
+            pltpu.VMEM((YR, SB, NAO), BF16),
+            pltpu.VMEM((YW, CHIPS, 16, KC), BF16),
+            pltpu.VMEM((YW, CHIPS, 16, KC), BF16),
+            pltpu.VMEM((WR, 2 * KC), BF16),
+            pltpu.VMEM((YW, NY - 1, WR, QC), BF16),
+            pltpu.VMEM((2, WR, QC), F32),
+            pltpu.VMEM((YW, NY - 1, WR, QC), BF16),
+            pltpu.VMEM((CHIPS, ZR, QC), F32),
+            pltpu.VMEM((ZW, CHIPS, ZR, QC), BF16),
+            pltpu.VMEM((ZW, CHIPS, ZR, QC), BF16),
+            pltpu.SMEM((2 * CHIPS + 16, 256), jnp.int32),
+            dma, dma((PW,)), dma((PW,)), dma, dma, dma((2,)), dma((YW,)), dma((YW,)), dma((YW,)), dma((YW,)), dma((ZW,)), dma((ZW,)), dma,
+        ],
+        compiler_params=pltpu.CompilerParams(collective_id=1, has_side_effects=True, vmem_limit_bytes=62 * 2**20),
+    )(tensor, block_mask, group_row, green_occ, green_virt)
+
+
+def shards(tensor, block_mask, group_of_block, green_occ, green_virt):
+    kept = jnp.sum(block_mask, axis=(1, 2)).reshape(NP // BS // 3, 3)
+    a, b, c = kept[:, 0], kept[:, 1], kept[:, 2]
+    most = jnp.max(jnp.maximum(jnp.maximum(3 * a, a + 2 * b), jnp.maximum(2 * b + c, 3 * c)))
+    return lax.cond(
+        most <= 2 * SLOTS, packed, whole, tensor, block_mask, group_of_block.reshape(1, 8), green_occ, green_virt
+    )
 
 
 def solution(mesh):

time: 169 us -> 147 us (0.87)
  Pallas kernels: 165 us -> 142 us
    pallas_call x1, Pallas kernels: 165 us -> 142 us  [packed(): pl.pallas_call(packed_kernel, out_shape=jax.ShapeDtypeStruct((ROWS, QC),...]
    unnamed x2 -> x1, local copies, waits for them, and re-layouts: 2.99 us -> 0.64 us
where the time goes in v3:
time: 147 us; the launch traced here: 146 us
  Pallas kernels  142 us (97%)
  local copies, waits for them, and re-layouts  2.19 us (1%)
  other arithmetic  1.5 us (1%)
    pallas_call x1, Pallas kernels, packed(): pl.pallas_call(packed_kernel, out_shape=jax.ShapeDtypeStruct((ROWS, QC),...  142 us

profile of v3, /device:TPU:0, one launch (start us, length us, event | category | flops | bytes accessed | tf_op | source)
XLA Modules:
  0.0 146.4 jit_solution(1257055238569594121)
XLA Ops:
  0.0 0.8 reduce_sum.9
  0.8 0.1 reshape.17
  0.9 0.7 maximum_reduce_fusion
  2.2 143.5 %conditional.1 = (f32[48,384]{1,0:T(8,128)S(1)}) conditional(s32[]{:T(128)} %convert_element_type.3, (bf16[48,512,512]{2,1,0:T(8,128)(2,1)}, s32[24,8,8]{0,2,1:T(8,128)}, s32[8]{0:T(128)}, bf16[512,512]{1,0:T(8,128)(2,1)}, bf16[512,512]{1,0:T(8,128)(2,1)}) %tuple.11, (bf16[48,512,512]{2,1,0:T(8,128)(2,1)}, s32[24,8,8]{0,2,1:T(8,128)}, s32[8]{0:T(128)}, ...), branch_computations={%region_2.0_spmd, %region_3.0_spmd} | conditional | bytes 12296 | solution.py:578
  2.4 1.5 %copy.19.mask = s32[24,8,8]{2,1,0:T(8,128)} copy(s32[24,8,8]{0,2,1:T(8,128)} %get-tuple-element.73) | data formatting | bytes 12288 | tf_op jit(solution)/shard_map
  3.9 141.8 %branch_1_fun.1 = f32[48,384]{1,0:T(8,128)S(1)} custom-call(bf16[48,512,512]{2,1,0:T(8,128)(2,1)} %get-tuple-element.48.tensor, s32[24,8,8]{2,1,0:T(8,128)} %copy.19.mask, s32[1,8]{1,0:T(1,128)} %bitcast.3, bf16[512,512]{1,0:T(8,128)(2,1)} %get-tuple-element.52.occ, bf16[512,512]{1,0:T(8,128)(2,1)} %get-tuple-element.54.virt), custom_call_target="tpu_custom_call" | custom-call | tf_op jit(solution)/shard_map/cond/branch_1_fun/pallas_call | solution.py:538
  145.7 0.6 copy.23

commit v4 on v3

--- a/solution.py
+++ b/solution.py
@@ -1,3 +1,5 @@
+import functools
+
 import jax
 import jax.numpy as jnp
 from jax import lax
@@ -32,8 +34,8 @@
 DY = (2, 1, 3)
 
 
-SLOTS = 60
-PW = 4
+TIERS = (42, 46, 52, 60)
+EARLY = (4, 10)
 UNITS = 3 * 64
 SR = 4
 
@@ -293,6 +295,21 @@
     )(tensor, block_mask, group_row, green_occ, green_virt)
 
 
+def granule_rows(chip, core):
+    odd = lax.rem(chip, 2)
+    gives = 2 - odd - core
+    first = jnp.where(gives == 0, 1, 0)
+    second = jnp.where(gives == 2, 1, 2)
+    row = chip * (2 * ROWS)
+    return row + core * ROWS + first * 16, row + core * ROWS + second * 16, row + (4 - 2 * core - odd) * 16, row + core * ROWS + gives * 16
+
+
+def slot_waves(slots):
+    late = slots - sum(EARLY)
+    third = late // 4 * 2
+    return *EARLY, third, late - third
+
+
 def dot(a, b):
     return jnp.dot(a, b, preferred_element_type=F32)
 
@@ -302,9 +319,10 @@
 
 
 def packed_kernel(
+    slots,
     tensor, mask, group, occ, virt, out,
-    xin, xs, xr, xl, tb, me, occ_f, occ_t, vm, perms, sel, tabs, own_pos, half, ys, yr, yl, cb, sb, yrs, zf, zb, zr, spots,
-    i_sem, x_send, x_recv, l_send, l_recv, t_sem, y_send, y_recv, c_send, c_recv, z_send, z_recv, s_sem,
+    xa, xb, xs, xr, xl, tb, me, occ_f, occ_t, vm, perms, sel, tabs, own_pos, half, ys, yr, yl, cb, sb, yrs, zf, zb, zr, spots,
+    i_sem, e_send, e_recv, x_send, x_recv, l_send, l_recv, t_sem, y_send, y_recv, c_send, c_recv, z_send, z_recv, s_sem,
 ):
     pa, mu = lax.axis_index("pa"), lax.axis_index("mu")
     x, z, core = pa // (2 * NZ), lax.rem(pa // 2, NZ), lax.rem(pa, 2)
@@ -331,15 +349,19 @@
     def tensor_chunk(w):
         return pltpu.make_async_copy(tensor.at[pl.ds(w * SR, SR)], tb.at[lax.rem(w, 2)], t_sem.at[lax.rem(w, 2)])
 
-    def load_x(u, carry):
-        g, a, b = u // 32, lax.rem(u // 4, 8), lax.rem(u, 4)
-        pltpu.make_async_copy(
-            tensor.at[pl.ds(g * 16, 16), pl.ds(pl.multiple_of(a * BS + mu * LB, LB), LB), pl.ds(pl.multiple_of(b * SB, SB), SB)],
-            xin.at[u], i_sem,
-        ).start()
-        return carry
-
-    lax.fori_loop(0, UNITS // 2, load_x, 0)
+    own_rows = granule_rows(chip, core)
+
+    def x_block(granule, v):
+        a, b = v // 4, lax.rem(v, 4)
+        row = pl.multiple_of(own_rows[granule] - pa * ROWS, 16)
+        return tensor.at[pl.ds(row, 16), pl.ds(pl.multiple_of(a * BS + mu * LB, LB), LB), pl.ds(pl.multiple_of(b * SB, SB), SB)]
+
+    def load_x(v, carry):
+        for g in (0, 1):
+            pltpu.make_async_copy(x_block(g, v), xa.at[g * 32 + v], i_sem).start()
+        return carry
+
+    lax.fori_loop(0, 32, load_x, 0)
     tensor_chunk(0).start()
     barrier = pltpu.get_barrier_semaphore()
     for dx, dz in NEAR:
@@ -347,28 +369,45 @@
     pl.semaphore_signal(barrier, inc=1, device_id=plane(x, z, 1 - core), device_id_type=MESH)
     for dy in DY:
         pl.semaphore_signal(barrier, inc=1, device_id=(pa, lax.rem(mu + dy, NY)), device_id_type=MESH)
-
-    flat = jnp.zeros((NP // BS, 64), F32)
-    for a in range(8):
-        place = (iota((8, 64), 1) == iota((8, 64), 0) + 8 * a).astype(F32)
-        flat += dot(mask[:, a, :].astype(F32), place)
+    pl.semaphore_wait(barrier, CHIPS + NY - 1)
+
+    def give_x(v, carry):
+        pltpu.make_async_remote_copy(
+            src_ref=x_block(3, v), dst_ref=xb.at[v], send_sem=e_send, recv_sem=e_recv,
+            device_id=plane(x, z, 1 - core), device_id_type=MESH,
+        ).start()
+        return carry
+
+    lax.fori_loop(0, 32, give_x, 0)
+
+    sizes = slot_waves(slots)
+    starts = [sum(sizes[:w]) for w in range(len(sizes))]
+
+    by_block = mask[...].astype(F32).reshape(64, NP // BS).astype(BF16)
     kept = jnp.zeros((2 * CHIPS, 256), F32)
     for g in range(3):
-        rows = ((iota((2 * CHIPS, NP // BS), 0) * ROWS + 16 * g) // BS == iota((2 * CHIPS, NP // BS), 1)).astype(F32)
-        place = (iota((64, 256), 1) == iota((64, 256), 0) + 64 * g).astype(F32)
-        kept += dot(dot(rows, flat), place)
-    upto = (iota((256, 256), 0) <= iota((256, 256), 1)).astype(F32)
-    place_of = dot(kept, upto)
+        device = iota((2 * CHIPS, NP // BS), 0)
+        first_row = granule_rows(device // 2, lax.rem(device, 2))[g]
+        rows = (first_row // BS == iota((2 * CHIPS, NP // BS), 1)).astype(F32).astype(BF16)
+        units = lax.dot_general(rows, by_block, (((1,), (1,)), ((), ())), preferred_element_type=F32).astype(BF16)
+        place = (iota((64, 256), 1) == iota((64, 256), 0) + 64 * g).astype(F32).astype(BF16)
+        kept += dot(units, place)
+    upto = (iota((256, 256), 0) <= iota((256, 256), 1)).astype(F32).astype(BF16)
+    place_of = dot(kept.astype(BF16), upto)
+    ours = jnp.sum(jnp.where(iota((2 * CHIPS, 256), 1) < 128, kept, 0.0), axis=1, keepdims=True)
+    place_of += jnp.where(iota((2 * CHIPS, 256), 1) < 128, 0.0, jnp.maximum(2 * sum(EARLY) - ours, 0.0))
     own_pos[...] = place_of * kept
     order = place_of.astype(jnp.int32) - 1
     odd = lax.rem(iota((2 * CHIPS, 256), 1), 2)
-    spot = order // 2 + jnp.where(lax.rem(order + 2, 2) == odd, 0, SLOTS)
-    tabs[0 : 2 * CHIPS] = jnp.clip(jnp.where(kept > 0.5, spot, 2 * SLOTS), 0, 2 * SLOTS)
-    taken = (own_pos[pl.ds(pa, 1), :] == (iota((256, 256), 0) + 1).astype(F32)).astype(F32)
-    units = iota((8, 256), 1).astype(F32)
+    spot = order // 2 + jnp.where(lax.rem(order + 2, 2) == odd, 0, slots)
+    tabs[0 : 2 * CHIPS] = jnp.clip(jnp.where(kept > 0.5, spot, 2 * slots), 0, 2 * slots)
+    taken = (own_pos[pl.ds(pa, 1), :] == (iota((256, 256), 0) + 1).astype(F32)).astype(F32).astype(BF16)
+    units = iota((8, 256), 1).astype(F32).astype(BF16)
     unit = lax.dot_general(units, taken, (((1,), (1,)), ((), ())), preferred_element_type=F32).astype(jnp.int32)
-    there = lax.dot_general(jnp.ones((8, 256), F32), taken, (((1,), (1,)), ((), ())), preferred_element_type=F32).astype(jnp.int32)
-    tabs[2 * CHIPS : 2 * CHIPS + 8] = jnp.clip(unit // 2, 0, UNITS // 2 - 1)
+    there = lax.dot_general(jnp.ones((8, 256), BF16), taken, (((1,), (1,)), ((), ())), preferred_element_type=F32).astype(jnp.int32)
+    tabs[2 * CHIPS : 2 * CHIPS + 8] = jnp.clip(unit // 2, 0, 63)
+    tabs[2 * CHIPS + 16 : 2 * CHIPS + 24] = unit // 128
+    tabs[2 * CHIPS + 24 : 2 * CHIPS + 32] = jnp.clip(unit // 2 - 64, 0, 31)
     tabs[2 * CHIPS + 8 : 2 * CHIPS + 16] = jnp.clip(there * (1 + lax.rem(unit, 2)), 0, 2)
     to_smem = pltpu.make_async_copy(tabs, spots, s_sem)
     to_smem.start()
@@ -385,30 +424,33 @@
     sel[3, 0] = (lax.rem(frm + BS, SB) == into).astype(BF16)
 
     to_smem.wait()
-    wait(xin, i_sem)
-    pl.semaphore_wait(barrier, CHIPS + NY - 1)
-
-    def pack(w, carry):
+    wait(xa, i_sem)
+
+    for w, n in enumerate(sizes):
+        if w == len(EARLY):
+            wait(xb, e_recv)
+
         def one(i, carry):
-            for k in range(3):
-                r = w * (SLOTS // PW) + i * 3 + k
+            for k in range(2):
+                r = starts[w] + i * 2 + k
                 full = jnp.zeros((256, SB), F32)
                 for h in (0, 1):
-                    cube = xin[spots[2 * CHIPS, 2 * r + h]].reshape(256, SB)
+                    cube = xa[spots[2 * CHIPS, 2 * r + h]]
+                    if w >= len(EARLY):
+                        cube = jnp.where(spots[2 * CHIPS + 16, 2 * r + h] > 0, xb[spots[2 * CHIPS + 24, 2 * r + h]], cube)
+                    cube = cube.reshape(256, SB)
                     full += dot(cube, sel[spots[2 * CHIPS + 8, 2 * r + h], h])
                 xs[:, r] = dot(perms[0], full.astype(BF16)).astype(BF16).reshape(16, 16, SB)
             return carry
 
-        lax.fori_loop(0, SLOTS // PW // 3, one, 0)
-        slots = pl.ds(w * (SLOTS // PW), SLOTS // PW)
-        to_chips(lambda t: xs.at[t, slots], xr.at[chip, slots], x_send.at[w], x_recv.at[w])
-        return carry
-
-    lax.fori_loop(0, PW, pack, 0)
+        lax.fori_loop(0, n // 2, one, 0)
+        part = pl.ds(starts[w], n)
+        to_chips(lambda t: xs.at[t, part], xr.at[chip, part], x_send.at[w], x_recv.at[w])
 
     spread = (block_of((NAO, 8), 0) == iota((NAO, 8), 1)).astype(F32)
     for g in range(3):
-        rows = dot(spread, mask[(ROWS * pa + 16 * g) // BS].astype(F32))
+        this = iota((8, 8, NP // BS), 2) == (ROWS * pa + 16 * g) // BS
+        rows = dot(spread, jnp.sum(jnp.where(this, mask[...].astype(F32), 0.0), axis=2))
         me[g] = lax.dot_general(rows, spread, (((1,), (1,)), ((), ())), preferred_element_type=F32).astype(BF16)
     group_row = group[...].astype(F32)
     row_group = jnp.sum(spread * group_row, axis=1, keepdims=True)
@@ -442,29 +484,28 @@
 
     lax.fori_loop(0, YW, make_product, 0)
 
-    for w in range(PW):
-        slots = pl.ds(w * (SLOTS // PW), SLOTS // PW)
-        wait(xr.at[:, slots], x_recv.at[w])
+    for w, n in enumerate(sizes):
+        wait(xr.at[:, pl.ds(starts[w], n)], x_recv.at[w])
     left_half = iota((16, SB), 1) < BS
 
     def unpack(i, carry):
-        rows = dot(xr[i, 0:SLOTS].reshape(SLOTS * 16, SB), sel[3, 0])
-        xr[i, SLOTS : 2 * SLOTS] = rows.astype(BF16).reshape(SLOTS, 16, SB)
-        xr[i, 2 * SLOTS] = jnp.zeros((16, SB), BF16)
+        rows = dot(xr[i, 0:slots].reshape(slots * 16, SB), sel[3, 0])
+        xr[i, slots : 2 * slots] = rows.astype(BF16).reshape(slots, 16, SB)
+        xr[i, 2 * slots] = jnp.zeros((16, SB), BF16)
         j = 2 * i + core
         for g in range(3):
-            row = pl.multiple_of(j * ROWS + g * 16, 16)
+            row = pl.multiple_of(granule_rows(i, core)[g], 16)
             for a in range(8):
                 for b in range(4):
                     u = (g * 8 + a) * 8 + 2 * b
                     both = jnp.where(left_half, xr[i, spots[j, u]], xr[i, spots[j, u + 1]])
                     first = a % 2 * KC + a // 2 * NAO + b * SB
                     xl[pl.ds(row, 16), first : first + SB] = both
-        rows = pl.ds(pl.multiple_of(j * ROWS, 16), ROWS)
-        pltpu.make_async_remote_copy(
-            src_ref=xl.at[rows], dst_ref=xl.at[rows], send_sem=l_send, recv_sem=l_recv,
-            device_id=plane(x, z, 1 - core), device_id_type=MESH,
-        ).start()
+            rows = pl.ds(row, 16)
+            pltpu.make_async_remote_copy(
+                src_ref=xl.at[rows], dst_ref=xl.at[rows], send_sem=l_send, recv_sem=l_recv,
+                device_id=plane(x, z, 1 - core), device_id_type=MESH,
+            ).start()
         return carry
 
     lax.fori_loop(0, CHIPS, unpack, 0)
@@ -522,9 +563,10 @@
 
     lax.fori_loop(0, ZW, finish, 0)
 
+    wait(xb, e_send)
     wait(xl.at[pl.ds(0, NP // 2)], l_send)
-    for w in range(PW):
-        wait(xs.at[pl.ds(0, CHIPS - 1), pl.ds(0, SLOTS // PW)], x_send.at[w])
+    for w, n in enumerate(sizes):
+        wait(xs.at[pl.ds(0, CHIPS - 1), pl.ds(0, n)], x_send.at[w])
     for w in range(YW):
         wait(yr.at[w, pl.ds(0, CHIPS - 1)], y_send.at[w])
         wait(cb.at[w], c_send.at[w])
@@ -532,18 +574,21 @@
         wait(zr.at[w, pl.ds(0, CHIPS - 1)], z_send.at[w])
 
 
-def packed(tensor, block_mask, group_row, green_occ, green_virt):
+def packed(tier, tensor, block_mask, group_row, green_occ, green_virt):
+    slots = TIERS[tier]
+    waves = len(slot_waves(slots))
     vmem = pl.BlockSpec(memory_space=pltpu.VMEM)
     dma = pltpu.SemaphoreType.DMA
     return pl.pallas_call(
-        packed_kernel,
+        functools.partial(packed_kernel, slots),
         out_shape=jax.ShapeDtypeStruct((ROWS, QC), F32),
         in_specs=[pl.BlockSpec(memory_space=pl.ANY), vmem, vmem, vmem, vmem],
         out_specs=vmem,
         scratch_shapes=[
-            pltpu.VMEM((UNITS // 2, 16, LB, SB), BF16),
-            pltpu.VMEM((CHIPS, SLOTS, 16, SB), BF16),
-            pltpu.VMEM((CHIPS, 2 * SLOTS + 1, 16, SB), BF16),
+            pltpu.VMEM((64, 16, LB, SB), BF16),
+            pltpu.VMEM((32, 16, LB, SB), BF16),
+            pltpu.VMEM((CHIPS, slots, 16, SB), BF16),
+            pltpu.VMEM((CHIPS, 2 * slots + 1, 16, SB), BF16),
             pltpu.VMEM((NP, 2 * KC), BF16),
             pltpu.VMEM((2, SR, NAO, NAO), BF16),
             pltpu.VMEM((3, NAO, NAO), BF16),
@@ -552,7 +597,7 @@
             pltpu.VMEM((NAO, NAO), BF16),
             pltpu.VMEM((3, 256, 256), BF16),
             pltpu.VMEM((4, 2, SB, SB), BF16),
-            pltpu.VMEM((2 * CHIPS + 16, 256), jnp.int32),
+            pltpu.VMEM((2 * CHIPS + 32, 256), jnp.int32),
             pltpu.VMEM((2 * CHIPS, 256), F32),
             pltpu.VMEM((YR, SB, NAO), BF16),
             pltpu.VMEM((YW, CHIPS, 16, KC), BF16),
@@ -564,20 +609,23 @@
             pltpu.VMEM((CHIPS, ZR, QC), F32),
             pltpu.VMEM((ZW, CHIPS, ZR, QC), BF16),
             pltpu.VMEM((ZW, CHIPS, ZR, QC), BF16),
-            pltpu.SMEM((2 * CHIPS + 16, 256), jnp.int32),
-            dma, dma((PW,)), dma((PW,)), dma, dma, dma((2,)), dma((YW,)), dma((YW,)), dma((YW,)), dma((YW,)), dma((ZW,)), dma((ZW,)), dma,
+            pltpu.SMEM((2 * CHIPS + 32, 256), jnp.int32),
+            dma, dma, dma, dma((waves,)), dma((waves,)), dma, dma, dma((2,)), dma((YW,)), dma((YW,)), dma((YW,)), dma((YW,)), dma((ZW,)), dma((ZW,)), dma,
         ],
-        compiler_params=pltpu.CompilerParams(collective_id=1, has_side_effects=True, vmem_limit_bytes=62 * 2**20),
-    )(tensor, block_mask, group_row, green_occ, green_virt)
+        compiler_params=pltpu.CompilerParams(collective_id=1 + tier, has_side_effects=True, vmem_limit_bytes=62 * 2**20),
+    )(tensor, jnp.transpose(block_mask, (1, 2, 0)), group_row, green_occ, green_virt)
 
 
 def shards(tensor, block_mask, group_of_block, green_occ, green_virt):
     kept = jnp.sum(block_mask, axis=(1, 2)).reshape(NP // BS // 3, 3)
     a, b, c = kept[:, 0], kept[:, 1], kept[:, 2]
-    most = jnp.max(jnp.maximum(jnp.maximum(3 * a, a + 2 * b), jnp.maximum(2 * b + c, 3 * c)))
-    return lax.cond(
-        most <= 2 * SLOTS, packed, whole, tensor, block_mask, group_of_block.reshape(1, 8), green_occ, green_virt
-    )
+    most = 0
+    for keeps, gets in ((2 * a, b), (a + b, a), (b + c, c), (2 * c, b)):
+        most = jnp.maximum(most, jnp.maximum(keeps, 2 * sum(EARLY)) + gets)
+    most = jnp.max(most)
+    branches = [functools.partial(packed, tier) for tier in range(len(TIERS))] + [whole]
+    which = sum((most > 2 * slots).astype(jnp.int32) for slots in TIERS)
+    return lax.switch(which, branches, tensor, block_mask, group_of_block.reshape(1, 8), green_occ, green_virt)
 
 
 def solution(mesh):

time: 147 us -> 143 us (0.973)
  Pallas kernels: 142 us -> 137 us
  between operations: 0.66 us -> 2.61 us
    pallas_call x1, Pallas kernels: 142 us -> 137 us  [packed(): pl.pallas_call(functools.partial(packed_kernel, slots), out_shape=jax.Sha...]
    another operation x1 -> x0, local copies, waits for them, and re-layouts: 1.47 us -> none
where the time goes in v4:
time: 143 us; the launch traced here: 142 us
  Pallas kernels  137 us (96%)
  between operations  2.61 us (2%)
  other arithmetic  1.43 us (1%)
    pallas_call x1, Pallas kernels, packed(): pl.pallas_call(functools.partial(packed_kernel, slots), out_shape=jax.Sha...  137 us

profile of v4, /device:TPU:0, one launch (start us, length us, event | category | flops | bytes accessed | tf_op | source)
XLA Modules:
  0.0 142.2 jit_solution(3919541329398730583)
XLA Ops:
  0.0 0.8 reduce_sum.9
  0.8 0.1 reshape.6
  0.9 0.2 slice_reduce_fusion.2
  1.1 0.6 maximum_reduce_fusion
  4.3 137.3 %conditional.1 = (f32[48,384]{1,0:T(8,128)S(1)}) conditional(s32[]{:T(128)} %clamp.3, (s32[24,8,8]{0,2,1:T(8,128)}, bf16[48,512,512]{2,1,0:T(8,128)(2,1)}, s32[1,8]{1,0:T(1,128)}, bf16[512,512]{1,0:T(8,128)(2,1)}, bf16[512,512]{1,0:T(8,128)(2,1)}) %tuple.36, (s32[24,8,8]{0,2,1:T(8,128)}, ...), branch_computations={%region_2.0_spmd, %region_3.0_spmd, %region_4.0_spmd, %region_5.0_... | conditional | bytes 12296 | solution.py:628
  4.5 136.7 %branch_2_fun.1 = f32[48,384]{1,0:T(8,128)S(1)} custom-call(bf16[48,512,512]{2,1,0:T(8,128)(2,1)} %get-tuple-element.71.tensor, s32[8,8,24]{2,1,0:T(8,128)} %bitcast.7, s32[1,8]{1,0:T(1,128)} %get-tuple-element.73.group, bf16[512,512]{1,0:T(8,128)(2,1)} %get-tuple-element.74.occ, bf16[512,512]{1,0:T(8,128)(2,1)} %get-tuple-element.75.virt), custom_call_target="tpu_custom_call" | custom-call | tf_op jit(solution)/shard_map/cond/branch_2_fun/pallas_call | solution.py:582
  141.6 0.6 copy.19

commit v5 on v4

--- a/solution.py
+++ b/solution.py
@@ -34,7 +34,7 @@
 DY = (2, 1, 3)
 
 
-TIERS = (42, 46, 52, 60)
+TIERS = (42, 46, 50, 56)
 EARLY = (4, 10)
 UNITS = 3 * 64
 SR = 4
@@ -622,9 +622,8 @@
     most = 0
     for keeps, gets in ((2 * a, b), (a + b, a), (b + c, c), (2 * c, b)):
         most = jnp.maximum(most, jnp.maximum(keeps, 2 * sum(EARLY)) + gets)
-    most = jnp.max(most)
     branches = [functools.partial(packed, tier) for tier in range(len(TIERS))] + [whole]
-    which = sum((most > 2 * slots).astype(jnp.int32) for slots in TIERS)
+    which = jnp.max(sum((most > 2 * slots).astype(jnp.int32) for slots in TIERS))
     return lax.switch(which, branches, tensor, block_mask, group_of_block.reshape(1, 8), green_occ, green_virt)
 
 

time: 143 us -> 137 us (0.958)
  Pallas kernels: 137 us -> 132 us
  between operations: 2.61 us -> 0.67 us
    pallas_call x1, Pallas kernels: 137 us -> 132 us  [packed(): pl.pallas_call(functools.partial(packed_kernel, slots), out_shape=jax.Sha...]
where the time goes in v5:
time: 137 us; the launch traced here: 136 us
  Pallas kernels  132 us (96%)
  other arithmetic  1.43 us (1%)
    pallas_call x1, Pallas kernels, packed(): pl.pallas_call(functools.partial(packed_kernel, slots), out_shape=jax.Sha...  132 us

profile of v5, /device:TPU:0, one launch (start us, length us, event | category | flops | bytes accessed | tf_op | source)
XLA Modules:
  0.0 135.5 jit_solution(11905749986175641997)
XLA Ops:
  0.0 0.8 reduce_sum.9
  0.8 0.1 reshape.6
  0.9 0.2 slice_reduce_fusion.2
  1.1 0.7 fusion.3
  2.4 132.5 %conditional.1 = (f32[48,384]{1,0:T(8,128)S(1)}) conditional(s32[]{:T(128)} %clamp.3, (s32[24,8,8]{0,2,1:T(8,128)}, bf16[48,512,512]{2,1,0:T(8,128)(2,1)}, s32[1,8]{1,0:T(1,128)}, bf16[512,512]{1,0:T(8,128)(2,1)}, bf16[512,512]{1,0:T(8,128)(2,1)}) %tuple.36, (s32[24,8,8]{0,2,1:T(8,128)}, ...), branch_computations={%region_2.0_spmd, %region_3.0_spmd, %region_4.0_spmd, %region_5.0_... | conditional | bytes 12296 | solution.py:627
  2.6 131.8 %branch_1_fun.1 = f32[48,384]{1,0:T(8,128)S(1)} custom-call(bf16[48,512,512]{2,1,0:T(8,128)(2,1)} %get-tuple-element.66.tensor, s32[8,8,24]{2,1,0:T(8,128)} %bitcast.6, s32[1,8]{1,0:T(1,128)} %get-tuple-element.68.group, bf16[512,512]{1,0:T(8,128)(2,1)} %get-tuple-element.69.occ, bf16[512,512]{1,0:T(8,128)(2,1)} %get-tuple-element.70.virt), custom_call_target="tpu_custom_call" | custom-call | tf_op jit(solution)/shard_map/cond/branch_1_fun/pallas_call | solution.py:582
  134.9 0.6 copy.19
